TPU v7x, 128 devices: a whole 4x4x4 slice. The times are simulated.
128 devices in a mesh: date: 4 (over y), tile: 32 (over x, z, core).
Axes of the slice: x: 4, y: 4, z: 4, core: 2. Of those that a mesh axis runs over, the one named last changes fastest.
Arguments:
- swath_intensities: bfloat16 [4, 512, 64, 2, 512], P('date', 'tile'), may hold values from 0.0099487305 to 1
- destination_patch: int32 [512, 1], P('tile'), may hold values from 0 to 31; in each aligned block of 16 rows (0 to 15, 16 to 31, ...) at most 2 rows name the same one
- swath_leading_scanline: int32 [512], P('tile'), may hold values from 0 to 64
- receiver_floor_intensity: float32 [4, 4096, 2, 512], P('date', 'tile'), may hold values from 0.1 to 1
Outputs:
- filtered: bfloat16 [4, 4096, 2, 512], P('date', 'tile')
Inputs may be any that keep to these rules, and one draw needn't show every extreme that they name: `destination_patch`: among the 16 blocks of one device no owner is named more than 2 times.
All inputs are finite; a program needn't handle non-finite values.
Results may differ from a plain program's by a relative error of at most 0.008.
Values may be sent and summed in bfloat16 or wider, within the bound.
A program may use at most 128 MiB of HBM per device.

v0:
```python
import jax
import jax.numpy as jnp
from jax import lax
from jax.sharding import PartitionSpec as P


def box_mean(field, row_axis, col_axis):
    total = field
    scale = jnp.ones((), jnp.float32)
    for axis in (row_axis, col_axis):
        length = field.shape[axis]
        widths = [(0, 0)] * field.ndim
        widths[axis] = (3, 3)
        padded = jnp.pad(total, widths)
        summed = lax.slice_in_dim(padded, 0, length, axis=axis)
        for shift_by in range(1, 7):
            summed = summed + lax.slice_in_dim(padded, shift_by, shift_by + length, axis=axis)
        total = summed
        places = jnp.arange(length, dtype=jnp.int32)
        counted = (jnp.minimum(places + 3, length - 1) - jnp.maximum(places - 3, 0) + 1).astype(
            jnp.float32
        )
        view = [1] * field.ndim
        view[axis] = length
        scale = scale * counted.reshape(view)
    return total / scale


def per_device(
    swath_intensities, destination_patch, swath_leading_scanline, receiver_floor_intensity
):
    swath_collection = swath_intensities[0]
    owners = destination_patch[:, 0]
    block_count = owners.shape[0]
    swath_scanlines = swath_collection.shape[1]
    raster_breadth_span = swath_collection.shape[3]
    tile_rows = receiver_floor_intensity.shape[1]
    first_rows = owners * tile_rows + swath_leading_scanline

    def insert_swath(swath_ordinal, scratch_matrix):
        destination_scanline = jnp.clip(
            first_rows[swath_ordinal] + swath_scanlines,
            0,
            tile_rows * lax.axis_size("tile") + swath_scanlines,
        )
        running_patch = lax.dynamic_slice_in_dim(
            scratch_matrix, destination_scanline, swath_scanlines, 0
        )
        return lax.dynamic_update_slice_in_dim(
            scratch_matrix,
            running_patch + swath_collection[swath_ordinal].astype(jnp.float32),
            destination_scanline,
            0,
        )

    scratch_matrix = lax.fori_loop(
        0,
        block_count,
        insert_swath,
        jnp.zeros(
            (tile_rows * lax.axis_size("tile") + 2 * swath_scanlines, 2, raster_breadth_span),
            jnp.float32,
        ),
    )
    raster_patch = lax.psum_scatter(
        scratch_matrix[
            swath_scanlines : swath_scanlines + tile_rows * lax.axis_size("tile")
        ].astype(jnp.bfloat16),
        "tile",
        scatter_dimension=0,
        tiled=True,
    ).astype(jnp.float32)
    raster_patch = raster_patch + receiver_floor_intensity[0]
    means = box_mean(raster_patch, 0, 2)
    ratio = raster_patch / means
    ratio_sum = lax.psum(ratio, "date") / lax.axis_size("date")
    return (means * ratio_sum).astype(jnp.bfloat16)[None]


def solution(mesh):
    return jax.shard_map(
        per_device,
        mesh=mesh,
        in_specs=(
            P("date", "tile", None, None, None),
            P("tile", None),
            P("tile"),
            P("date", "tile", None, None),
        ),
        out_specs=P("date", "tile", None, None),
        check_vma=False,
    )
```

profile of v0, /device:TPU:0, one launch (start us, length us, event | category | flops | bytes accessed | tf_op | source)
XLA Modules:
  0.0 251.6 jit_solution(8482926227587942734)
XLA Ops:
  6.5 0.0 all-reduce.8.cloned.1.call-start
  6.5 0.7 bitcast_add_fusion.1
  7.2 6.2 %broadcast_in_dim.6 = f32[4224,2,512]{2,1,0:T(2,128)} broadcast(f32[]{:T(128)} %constant.59.clone.1), dimensions={} | broadcast | bytes 17301508 | tf_op jit(solution)/shard_map/broadcast_in_dim | solution.py:60
  13.4 0.0 copy-start.1
  13.4 0.0 copy-start
  13.4 47.4 %while.13 = (s32[]{:T(128)}, f32[4224,2,512]{2,1,0:T(2,128)}, s32[16]{0:T(128)S(1)}, bf16[16,64,2,512]{3,2,1,0:T(2,128)(2,1)}, s32[]{:T(128)}, /*index=5*/s32[1]{0:T(128)}, s32[1]{0:T(128)}, s32[1]{0:T(128)}) while((s32[]{:T(128)}, f32[4224,2,512]{2,1,0:T(2,128)}, s32[16]{0:T(128)S(1)}, bf16[16,64,2,512]{3,2,1,0:T(2,128)(2,1)}, s32[]{:T(128)}, ...), condition=%wide.region_1.2_spmd, body=%wide.region_0.1_spmd.sunk | while | flops 131077 | bytes 656517 | solution.py:56
  13.4 0.6 dynamic_slice.28
  14.6 1.8 fusion.16
  16.4 0.6 dynamic_slice.28
  17.5 1.8 fusion.16
  19.3 0.6 dynamic_slice.28
  20.5 1.8 fusion.16
  22.3 0.6 dynamic_slice.28
  23.4 1.8 fusion.16
  25.3 0.6 dynamic_slice.28
  26.4 1.8 fusion.16
  28.2 0.6 dynamic_slice.28
  29.3 1.8 fusion.16
  31.2 0.6 dynamic_slice.28
  32.3 1.9 fusion.16
  34.2 0.6 dynamic_slice.28
  35.3 1.8 fusion.16
  37.1 0.6 dynamic_slice.28
  38.3 1.8 fusion.16
  40.1 0.6 dynamic_slice.28
  41.2 1.8 fusion.16
  43.1 0.6 dynamic_slice.28
  44.2 1.8 fusion.16
  46.0 0.6 dynamic_slice.28
  47.2 1.8 fusion.16
  49.0 0.6 dynamic_slice.28
  50.1 1.8 fusion.16
  52.0 0.6 dynamic_slice.28
  53.1 1.8 fusion.16
  54.9 0.6 dynamic_slice.28
  56.1 1.8 fusion.16
  57.9 0.6 dynamic_slice.28
  59.0 1.8 fusion.16
  60.9 9.4 %slice.81 = bf16[4096,2,512]{2,1,0:T(2,128)(2,1)} slice(f32[4224,2,512]{2,1,0:T(2,128)} %get-tuple-element.84), slice={[64:4160], [0:2], [0:512]} | slice | bytes 16777216 | tf_op jit(solution)/shard_map/slice | solution.py:66
  70.3 0.0 all-reduce.8.cloned.1.call-update
  70.3 0.0 all-reduce.6.cloned.1.call-start
  70.3 0.0 copy-done.1
  70.4 0.6 dynamic-slice
  71.6 0.1 broadcast_multiply_fusion
  71.7 122.6 %all-reduce.8.cloned.1.call-done = bf16[4096,2,512]{2,1,0:T(2,128)(2,1)} async-done(((bf16[4096,2,512]{2,1,0:T(2,128)(2,1)}), bf16[4096,2,512]{2,1,0:T(2,128)(2,1)}) %all-reduce.8.cloned.1.call-update) | async-done | bytes 8388624
  194.3 0.0 copy-done
  194.3 1.2 bitcast_add_fusion
  195.5 0.4 slice_add_fusion.1
  195.9 4.1 %multiply_divide_fusion = (f32[128,2,512]{2,1,0:T(2,128)}, f32[128,2,512]{2,1,0:T(2,128)S(1)}) fusion(f32[128,2,512]{2,1,0:T(2,128)S(1)} %bitcast_add_fusion, f32[128,512]{1,0:T(8,128)S(1)} %broadcast_multiply_fusion, f32[128,2,512]{2,1,0:T(2,128)S(1)} %slice_add_fusion.1), kind=kLoop, calls=%fused_computation.5 | loop fusion | flops 1048576 | bytes 2359296 | tf_op jit(solution)/shard_map/div | solution.py:75
  200.1 0.0 all-reduce.6.cloned.1.call-update
  200.1 42.5 %all-reduce.6.cloned.1.call-done = f32[128,2,512]{2,1,0:T(2,128)} async-done(((f32[128,2,512]{2,1,0:T(2,128)}), f32[128,2,512]{2,1,0:T(2,128)}) %all-reduce.6.cloned.1.call-update) | async-done | bytes 524304 | tf_op jit(solution)/shard_map/psum | solution.py:76
  242.6 2.2 fusion.4
  (2 shorter events, 0.0 us)
Async XLA Ops:
  6.5 187.7 %all-reduce.8.cloned.1.call-start = ((), (), s32[]{:S(2)}) async-start(), calls=%async_computation.1 | async-start | bytes 16777216
  13.4 56.9 %copy-start.1 = (u32[128]{0:T(128)S(1)}, u32[128]{0:T(128)}, u32[]{:S(2)}) copy-start(u32[128]{0:T(128)} %constant.77) | copy-start | bytes 1540
  13.4 180.9 %copy-start = (f32[1,128,2,512]{3,2,1,0:T(2,128)S(1)}, f32[1,128,2,512]{3,2,1,0:T(2,128)}, u32[]{:S(2)}) copy-start(f32[1,128,2,512]{3,2,1,0:T(2,128)} %param.9) | copy-start | bytes 1572868
  70.3 172.3 %all-reduce.6.cloned.1.call-start = ((), (), s32[]{:S(2)}) async-start(), calls=%async_computation | async-start | bytes 1048576 | tf_op jit(solution)/shard_map/psum | solution.py:76
Sparse Core Ops, SparseCore 0:
  70.4 123.8 all-reduce.7
  200.2 42.3 all-reduce.5
where the time goes:
time: 252 us
  waiting for transfers between devices  165 us (65%)
  other arithmetic  38 us (15%)
  local copies, waits for them, and re-layouts  25.1 us (10%)
  between operations  14.1 us (6%)
  loops' own time  9.24 us (4%)
    unnamed x3, waiting for transfers between devices  123 us
    psum x1, waiting for transfers between devices, per_device(): ratio_sum = lax.psum(ratio, 'date') / lax.axis_size('date')  42.5 us
    dynamic_update_slice x16, other arithmetic, insert_swath(): lax.dynamic_update_slice_in_dim(scratch_matrix, running_patch + swath_col...  29.3 us
    slice x1, local copies, waits for them, and re-layouts, per_device(): scratch_matrix[swath_scanlines:swath_scanlines + tile_rows * lax.axis_siz...  9.41 us
    another operation x1, loops' own time, per_device(): lax.fori_loop(0, block_count, insert_swath, jnp.zeros((tile_rows * lax.ax...  9.24 us
    dynamic_slice x16, local copies, waits for them, and re-layouts, insert_swath(): first_rows[swath_ordinal] + swath_scanlines  8.88 us
    broadcast_in_dim x1, local copies, waits for them, and re-layouts, per_device(): jnp.zeros((tile_rows * lax.axis_size('tile') + 2 * swath_scanlines, 2, ra...  6.2 us
  transfers between devices with their start and end apart: 2, of which 2 were waited for; matrix products, arithmetic and copies ran while one was open for 0% of the time, Pallas kernels for 0%

commit v1 on v0

v1 whole, which is shorter than its diff:
```python
import functools

import jax
import jax.numpy as jnp
from jax import lax
from jax.experimental import pallas as pl
from jax.experimental.pallas import tpu as pltpu
from jax.sharding import PartitionSpec as P

MESH = pl.DeviceIdType.MESH
RING = 4
BOUNDS = (0, 32, 64, 96, 128)
LAG = 4
HALF = 3
GROUPS = (2, 1, 3, 0)
CHUNK = 16
FILTER_CHUNK = 4


def owner_of(first, second, core):
    x = first * (1 - core) + second * core
    z = second * (1 - core) + first * core
    return (x * RING + z) * 2 + core


def shift_columns(rows, by):
    lane = lax.broadcasted_iota(jnp.int32, rows.shape, 2)
    sub = lax.broadcasted_iota(jnp.int32, rows.shape, 1)
    turned = pltpu.roll(rows, by % 128, 2)
    if by > 0:
        beside = jnp.where(sub < 2, 0.0, pltpu.roll(turned, 2, 1))
        return jnp.where(lane < by, beside, turned)
    beside = jnp.where(sub >= 6, 0.0, pltpu.roll(turned, 6, 1))
    return jnp.where(lane >= 128 + by, beside, turned)


def kernel(
    blocks, block_rows, tile_rows, n_tile,
    swath, dest, lead, floor, out,
    raw, table, xs, xr, a1s, a1r, a2s, a2r, b2s, b2r, bs, br, canvas, means, own_ratio, ds_, dr,
    raw_sem, floor_sem, x_ss, x_rs, a1_ss, a1_rs, a2_ss, a2_rs, b2_ss, b2_rs, b_ss, b_rs, d_ss, d_rs,
):
    bf16, f32 = jnp.bfloat16, jnp.float32
    tile, date = lax.axis_index("tile"), lax.axis_index("date")
    core = tile % 2
    x, z = tile // (2 * RING), (tile // 2) % RING
    a = x * (1 - core) + z * core
    b = z * (1 - core) + x * core
    pieces = len(BOUNDS) - 1
    stride = tile_rows
    pad = stride - block_rows

    loads = [
        pltpu.make_async_copy(
            swath.at[pl.ds(i * block_rows, block_rows)],
            raw.at[pl.ds(i * stride + pad, block_rows)],
            raw_sem.at[i],
        )
        for i in range(blocks)
    ]
    for copy in loads:
        copy.start()
    floor_copy = pltpu.make_async_copy(floor, canvas.at[pl.ds(HALF, tile_rows)], floor_sem)
    floor_copy.start()

    partner = (date, owner_of(b, a, 1 - core))
    ahead = (date, owner_of((a + 1) % RING, b, core))
    behind = (date, owner_of((a + RING - 1) % RING, b, core))
    across = [(date, owner_of(a, (b + j) % RING, core)) for j in (1, 2, 3)]
    dates = [((date + j) % RING, tile) for j in (1, 2, 3)]
    barrier = pltpu.get_barrier_semaphore()
    everyone = [partner, ahead, behind] + across + dates
    for device in everyone:
        pl.semaphore_signal(barrier, inc=1, device_id=device, device_id_type=MESH)

    def clear(i, _):
        raw[pl.ds(i * stride, pad)] = jnp.zeros((pad, 8, 128), bf16)
        return 0

    lax.fori_loop(0, blocks, clear, 0)
    raw[pl.ds(blocks * stride, tile_rows)] = jnp.zeros((tile_rows, 8, 128), bf16)
    canvas[pl.ds(0, HALF)] = jnp.zeros((HALF, 8, 128), f32)
    canvas[pl.ds(HALF + tile_rows, HALF)] = jnp.zeros((HALF, 8, 128), f32)

    names = [dest[i] for i in range(blocks)]
    starts = [i * stride + pad - jnp.clip(lead[i], 0, pad) for i in range(blocks)]
    empty = blocks * stride

    def fill(o, _):
        least, second = jnp.int32(empty), jnp.int32(empty)
        for i in range(blocks):
            here = jnp.where(names[i] == o, starts[i], empty)
            second = jnp.minimum(second, jnp.maximum(least, here))
            least = jnp.minimum(least, here)
        table[2 * o] = least
        table[2 * o + 1] = second
        return 0

    lax.fori_loop(0, n_tile, fill, 0)

    for copy in loads:
        copy.wait()
    pl.semaphore_wait(barrier, len(everyone))

    sent = []

    def send(src, dst, ss, rs, device):
        copy = pltpu.make_async_remote_copy(
            src_ref=src, dst_ref=dst, send_sem=ss, recv_sem=rs, device_id=device, device_id_type=MESH
        )
        copy.start()
        sent.append(copy)
        return copy

    def spread(first, count, p, owner, store):
        low, high = BOUNDS[p], BOUNDS[p + 1]
        chunks = (high - low) // CHUNK

        def one(i, _):
            j = first + i // chunks
            row = low + (i % chunks) * CHUNK
            o = owner(j)
            one_, two_ = table[2 * o], table[2 * o + 1]
            total = raw[pl.ds(one_ + row, CHUNK)].astype(f32) + raw[pl.ds(two_ + row, CHUNK)].astype(f32)
            store(j, pl.ds(row, CHUNK), total)
            return 0

        lax.fori_loop(0, count * chunks, one, 0)

    x_copies, a1_copies, a2_copies, b2_copies, b_copies, d_copies = {}, {}, {}, {}, {}, {}

    def rows_of(p):
        return pl.ds(BOUNDS[p], BOUNDS[p + 1] - BOUNDS[p])

    def mine(step):
        return lambda j: owner_of((a + step) % RING, (b + j) % RING, core)

    def to_partner(p):
        for g, step in enumerate(GROUPS):

            def keep(j, rows, total):
                xs[g, j, rows] = total.astype(bf16)

            spread(0, RING, p, lambda j: owner_of((b + step) % RING, (a + j) % RING, 1 - core), keep)
            k = p * RING + g
            x_copies[p, g] = send(
                xs.at[g, :, rows_of(p)], xr.at[g, :, rows_of(p)], x_ss.at[k], x_rs.at[k], partner
            )

    def first_sends(p):
        x_copies[p, 0].wait_recv()

        def keep(j, rows, total):
            a1s[j, rows] = (total + xr[0, j, rows].astype(f32)).astype(bf16)

        spread(0, RING, p, mine(2), keep)
        for way, device in enumerate((ahead, behind)):
            k = p * 2 + way
            part = pl.ds(2 * way, 2)
            a1_copies[p, way] = send(
                a1s.at[part, rows_of(p)], a1r.at[part, rows_of(p)], a1_ss.at[k], a1_rs.at[k], device
            )
        for way, device in enumerate((ahead, behind)):
            g = 1 + way
            x_copies[p, g].wait_recv()

            def keep_far(j, rows, total):
                a2s[j, rows] = (total + xr[g, j, rows].astype(f32)).astype(bf16)

            spread(2 - 2 * way, 2, p, mine(GROUPS[g]), keep_far)
            k = p * 2 + way
            part = pl.ds(2 - 2 * way, 2)
            a2_copies[p, way] = send(
                a2s.at[part, rows_of(p)], a2r.at[part, rows_of(p)], a2_ss.at[k], a2_rs.at[k], device
            )

    def second_sends(p):
        for way, device in enumerate((ahead, behind)):
            g = 1 + way
            a1_copies[p, way].wait_recv()

            def keep(j, rows, total):
                total = total + xr[g, j, rows].astype(f32) + a1r[j, rows].astype(f32)
                b2s[j, rows] = total.astype(bf16)

            spread(2 * way, 2, p, mine(GROUPS[g]), keep)
            k = p * 2 + way
            part = pl.ds(2 * way, 2)
            b2_copies[p, way] = send(
                b2s.at[part, rows_of(p)], b2r.at[part, rows_of(p)], b2_ss.at[k], b2_rs.at[k], device
            )

    def cross(p):
        x_copies[p, 3].wait_recv()
        for way in range(2):
            a2_copies[p, way].wait_recv()
            b2_copies[p, way].wait_recv()

        def summed(j, rows, total):
            total = total + xr[3, j, rows].astype(f32)
            return total + a2r[j, rows].astype(f32) + b2r[j, rows].astype(f32)

        def keep(j, rows, total):
            bs[j - 1, rows] = summed(j, rows, total).astype(bf16)

        def keep_own(j, rows, total):
            here = pl.ds(HALF + rows.start, CHUNK)
            canvas[here] += summed(0, rows, total)

        spread(1, RING - 1, p, mine(0), keep)
        for j in (2, 1, 3):
            k = p * 3 + j - 1
            b_copies[p, j] = send(
                bs.at[j - 1, rows_of(p)], br.at[j - 1, rows_of(p)], b_ss.at[k], b_rs.at[k], across[j - 1]
            )
        if p == 0:
            floor_copy.wait()
        spread(0, 1, p, mine(0), keep_own)

    def filtered_rows(p):
        low = max(0, BOUNDS[p] - LAG)
        high = tile_rows if p == pieces - 1 else BOUNDS[p + 1] - LAG
        return low, high

    def box(p):
        for j in (1, 2, 3):
            b_copies[p, j].wait_recv()
        low, high = BOUNDS[p], BOUNDS[p + 1]

        def add(i, _):
            row = low + i * CHUNK
            rows = pl.ds(row, CHUNK)
            canvas[pl.ds(HALF + row, CHUNK)] += (
                br[0, rows].astype(f32) + br[1, rows].astype(f32) + br[2, rows].astype(f32)
            )
            return 0

        lax.fori_loop(0, (high - low) // CHUNK, add, 0)
        low, high = filtered_rows(p)
        shape = (FILTER_CHUNK, 8, 128)
        column = (lax.broadcasted_iota(jnp.int32, shape, 1) // 2) * 128 + lax.broadcasted_iota(jnp.int32, shape, 2)
        last = 4 * 128 - 1
        wide = jnp.minimum(column + HALF, last) - jnp.maximum(column - HALF, 0) + 1
        wide = wide.astype(f32)

        def smooth(i, _):
            row = low + i * FILTER_CHUNK
            total = canvas[pl.ds(row, FILTER_CHUNK)]
            for k in range(1, 2 * HALF + 1):
                total = total + canvas[pl.ds(row + k, FILTER_CHUNK)]
            summed = total
            for k in range(1, HALF + 1):
                summed = summed + (shift_columns(total, k) + shift_columns(total, -k))
            at = row + lax.broadcasted_iota(jnp.int32, shape, 0)
            tall = jnp.minimum(at + HALF, tile_rows - 1) - jnp.maximum(at - HALF, 0) + 1
            mean = summed / (tall.astype(f32) * wide)
            ratio = canvas[pl.ds(row + HALF, FILTER_CHUNK)] / mean
            rows = pl.ds(row, FILTER_CHUNK)
            means[rows] = mean
            own_ratio[rows] = ratio
            ds_[rows] = ratio.astype(bf16)
            return 0

        lax.fori_loop(0, (high - low) // FILTER_CHUNK, smooth, 0)
        rows = pl.ds(low, high - low)
        for j in (2, 1, 3):
            k = p * 3 + j - 1
            d_copies[p, j] = send(ds_.at[rows], dr.at[j - 1, rows], d_ss.at[k], d_rs.at[k], dates[j - 1])

    def finish(p):
        for j in (1, 2, 3):
            d_copies[p, j].wait_recv()
        low, high = filtered_rows(p)

        def one(i, _):
            rows = pl.ds(low + i * FILTER_CHUNK, FILTER_CHUNK)
            total = own_ratio[rows] + dr[0, rows].astype(f32)
            total = total + (dr[1, rows].astype(f32) + dr[2, rows].astype(f32))
            out[rows] = (means[rows] * (total * (1.0 / RING))).astype(bf16)
            return 0

        lax.fori_loop(0, (high - low) // FILTER_CHUNK, one, 0)

    stages = (to_partner, first_sends, second_sends, cross, box, finish)
    for t in range(pieces + len(stages) - 1):
        for s, stage in enumerate(stages):
            if 0 <= t - s < pieces:
                stage(t - s)
    for copy in sent:
        copy.wait_send()


def per_device(swath_intensities, destination_patch, swath_leading_scanline, receiver_floor_intensity):
    _, blocks, block_rows, pols, width = swath_intensities.shape
    tile_rows = receiver_floor_intensity.shape[1]
    n_tile = lax.axis_size("tile")
    cols = width // 128

    def rowwise(array, rows):
        return array.reshape(rows, pols, cols, 128).transpose(0, 2, 1, 3).reshape(rows, pols * cols, 128)

    pieces = len(BOUNDS) - 1
    bf16, f32 = jnp.bfloat16, jnp.float32

    def buffer(*lead, dtype=bf16):
        return pltpu.VMEM((*lead, 8, 128), dtype)

    dma = pltpu.SemaphoreType.DMA
    scratch = [
        buffer(blocks * tile_rows + tile_rows),
        pltpu.SMEM((2 * n_tile,), jnp.int32),
        buffer(4, 4, tile_rows), buffer(4, 4, tile_rows),
        buffer(4, tile_rows), buffer(4, tile_rows),
        buffer(4, tile_rows), buffer(4, tile_rows),
        buffer(4, tile_rows), buffer(4, tile_rows),
        buffer(3, tile_rows), buffer(3, tile_rows),
        buffer(tile_rows + 2 * HALF, dtype=f32),
        buffer(tile_rows, dtype=f32), buffer(tile_rows, dtype=f32),
        buffer(tile_rows), buffer(3, tile_rows),
        dma((blocks,)), dma,
        dma((pieces * 4,)), dma((pieces * 4,)),
        dma((pieces * 2,)), dma((pieces * 2,)),
        dma((pieces * 2,)), dma((pieces * 2,)),
        dma((pieces * 2,)), dma((pieces * 2,)),
        dma((pieces * 3,)), dma((pieces * 3,)),
        dma((pieces * 3,)), dma((pieces * 3,)),
    ]
    filtered = pl.pallas_call(
        functools.partial(kernel, blocks, block_rows, tile_rows, n_tile),
        out_shape=jax.ShapeDtypeStruct((tile_rows, pols * cols, 128), bf16),
        in_specs=[
            pl.BlockSpec(memory_space=pl.ANY),
            pl.BlockSpec(memory_space=pltpu.SMEM),
            pl.BlockSpec(memory_space=pltpu.SMEM),
            pl.BlockSpec(memory_space=pl.ANY),
        ],
        out_specs=pl.BlockSpec(memory_space=pltpu.VMEM),
        scratch_shapes=scratch,
        compiler_params=pltpu.CompilerParams(
            collective_id=0, has_side_effects=True, vmem_limit_bytes=60 << 20
        ),
        name="quegan",
    )(
        rowwise(swath_intensities, blocks * block_rows),
        destination_patch[:, 0],
        swath_leading_scanline,
        rowwise(receiver_floor_intensity, tile_rows),
    )
    return filtered.reshape(tile_rows, cols, pols, 128).transpose(0, 2, 1, 3).reshape(1, tile_rows, pols, width)


def solution(mesh):
    return jax.shard_map(
        per_device,
        mesh=mesh,
        in_specs=(
            P("date", "tile", None, None, None),
            P("tile", None),
            P("tile"),
            P("date", "tile", None, None),
        ),
        out_specs=P("date", "tile", None, None),
        check_vma=False,
    )
```

time: 252 us -> 48.3 us (0.19)
  waiting for transfers between devices: 165 us -> 0 us
  Pallas kernels: 0 us -> 46.3 us
  other arithmetic: 38 us -> 0 us
  local copies, waits for them, and re-layouts: 25.1 us -> 1.83 us
  between operations: 14.1 us -> 0.01 us
  loops' own time: 9.24 us -> 0 us
    unnamed x3 -> x0, waiting for transfers between devices: 123 us -> none
    pallas_call x0 -> x1, Pallas kernels: none -> 46.3 us  [per_device(): pl.pallas_call(functools.partial(kernel, blocks, block_rows, tile_rows, n...]
    psum x1 -> x0, waiting for transfers between devices: 42.5 us -> none  [per_device(): ratio_sum = lax.psum(ratio, 'date') / lax.axis_size('date')]
    dynamic_update_slice x16 -> x0, other arithmetic: 29.3 us -> none  [insert_swath(): lax.dynamic_update_slice_in_dim(scratch_matrix, running_patch + swath_col...]
    slice x1 -> x0, local copies, waits for them, and re-layouts: 9.41 us -> none  [per_device(): scratch_matrix[swath_scanlines:swath_scanlines + tile_rows * lax.axis_siz...]
    another operation x1 -> x0, loops' own time: 9.24 us -> none  [per_device(): lax.fori_loop(0, block_count, insert_swath, jnp.zeros((tile_rows * lax.ax...]
    dynamic_slice x16 -> x0, local copies, waits for them, and re-layouts: 8.88 us -> none  [insert_swath(): first_rows[swath_ordinal] + swath_scanlines]
    broadcast_in_dim x1 -> x0, local copies, waits for them, and re-layouts: 6.2 us -> none  [per_device(): jnp.zeros((tile_rows * lax.axis_size('tile') + 2 * swath_scanlines, 2, ra...]
  transfers between devices with their start and end apart: 2 -> 0, of which waited for: 2 -> 0; matrix products, arithmetic and copies ran while one was open for 0% -> 0% of each run, Pallas kernels for 0% -> 0%
where the time goes in v1:
time: 48.3 us; the launch traced here: 48.2 us
  Pallas kernels  46.3 us (96%)
  local copies, waits for them, and re-layouts  1.83 us (4%)
    pallas_call x1, Pallas kernels, per_device(): pl.pallas_call(functools.partial(kernel, blocks, block_rows, tile_rows, n...  46.3 us
    unnamed x1, local copies, waits for them, and re-layouts  1.83 us

profile of v1, /device:TPU:0, one launch (start us, length us, event | category | flops | bytes accessed | tf_op | source)
XLA Modules:
  0.0 48.2 jit_solution(18358743112545468662)
XLA Ops:
  0.0 46.3 %quegan.1 = bf16[128,8,128]{2,1,0:T(8,128)(2,1)} custom-call(bf16[1024,8,128]{2,1,0:T(8,128)(2,1)} %bitcast.16, s32[16]{0:T(128)} %bitcast.19, s32[16]{0:T(128)} %lead.1, f32[128,8,128]{2,1,0:T(8,128)} %bitcast.18), custom_call_target="tpu_custom_call" | custom-call | tf_op jit(solution)/shard_map/quegan/pallas_call | solution.py:328
  46.3 1.8 %copy.9 = bf16[1,128,2,512]{3,2,1,0:T(2,128)(2,1)} copy(bf16[1,128,2,512]{3,2,1,0:T(2,128)(2,1)} %bitcast.17) | data formatting | bytes 524288

commit v2 on v1

--- a/solution.py
+++ b/solution.py
@@ -9,7 +9,9 @@
 
 MESH = pl.DeviceIdType.MESH
 RING = 4
-BOUNDS = (0, 32, 64, 96, 128)
+BOUNDS = (0, 16, 32, 48, 64, 80, 96, 112, 128)
+LAGS = (0, 1, 4, 7, 9.5, 20)
+FIRST = True
 LAG = 4
 HALF = 3
 GROUPS = (2, 1, 3, 0)
@@ -37,8 +39,8 @@
 def kernel(
     blocks, block_rows, tile_rows, n_tile,
     swath, dest, lead, floor, out,
-    raw, table, xs, xr, a1s, a1r, a2s, a2r, b2s, b2r, bs, br, canvas, means, own_ratio, ds_, dr,
-    raw_sem, floor_sem, x_ss, x_rs, a1_ss, a1_rs, a2_ss, a2_rs, b2_ss, b2_rs, b_ss, b_rs, d_ss, d_rs,
+    raw, windows, table, xs, xr, as_, ar, b2s, b2r, bs, br, canvas, means, own_ratio, ds_, dr,
+    raw_sem, table_sem, floor_sem, x_ss, x_rs, a_ss, a_rs, b2_ss, b2_rs, b_ss, b_rs, d_ss, d_rs,
 ):
     bf16, f32 = jnp.bfloat16, jnp.float32
     tile, date = lax.axis_index("tile"), lax.axis_index("date")
@@ -49,6 +51,16 @@
     pieces = len(BOUNDS) - 1
     stride = tile_rows
     pad = stride - block_rows
+
+    partner = (date, owner_of(b, a, 1 - core))
+    ahead = (date, owner_of((a + 1) % RING, b, core))
+    behind = (date, owner_of((a + RING - 1) % RING, b, core))
+    across = [(date, owner_of(a, (b + j) % RING, core)) for j in (1, 2, 3)]
+    dates = [((date + j) % RING, tile) for j in (1, 2, 3)]
+    barrier = pltpu.get_barrier_semaphore()
+    everyone = [partner, ahead, behind] + across + dates
+    for device in everyone:
+        pl.semaphore_signal(barrier, inc=1, device_id=device, device_id_type=MESH)
 
     loads = [
         pltpu.make_async_copy(
@@ -63,15 +75,21 @@
     floor_copy = pltpu.make_async_copy(floor, canvas.at[pl.ds(HALF, tile_rows)], floor_sem)
     floor_copy.start()
 
-    partner = (date, owner_of(b, a, 1 - core))
-    ahead = (date, owner_of((a + 1) % RING, b, core))
-    behind = (date, owner_of((a + RING - 1) % RING, b, core))
-    across = [(date, owner_of(a, (b + j) % RING, core)) for j in (1, 2, 3)]
-    dates = [((date + j) % RING, tile) for j in (1, 2, 3)]
-    barrier = pltpu.get_barrier_semaphore()
-    everyone = [partner, ahead, behind] + across + dates
-    for device in everyone:
-        pl.semaphore_signal(barrier, inc=1, device_id=device, device_id_type=MESH)
+    names = [dest[i] for i in range(blocks)]
+    starts = [i * stride + pad - jnp.clip(lead[i], 0, pad) for i in range(blocks)]
+    empty = blocks * stride
+
+    owner = lax.broadcasted_iota(jnp.int32, (8, 128), 1)
+    least = jnp.full((8, 128), empty, jnp.int32)
+    other = least
+    for i in range(blocks):
+        here = jnp.where(owner == names[i], starts[i], empty)
+        other = jnp.minimum(other, jnp.maximum(least, here))
+        least = jnp.minimum(least, here)
+    windows[0] = least
+    windows[1] = other
+    table_copy = pltpu.make_async_copy(windows, table, table_sem)
+    table_copy.start()
 
     def clear(i, _):
         raw[pl.ds(i * stride, pad)] = jnp.zeros((pad, 8, 128), bf16)
@@ -82,22 +100,7 @@
     canvas[pl.ds(0, HALF)] = jnp.zeros((HALF, 8, 128), f32)
     canvas[pl.ds(HALF + tile_rows, HALF)] = jnp.zeros((HALF, 8, 128), f32)
 
-    names = [dest[i] for i in range(blocks)]
-    starts = [i * stride + pad - jnp.clip(lead[i], 0, pad) for i in range(blocks)]
-    empty = blocks * stride
-
-    def fill(o, _):
-        least, second = jnp.int32(empty), jnp.int32(empty)
-        for i in range(blocks):
-            here = jnp.where(names[i] == o, starts[i], empty)
-            second = jnp.minimum(second, jnp.maximum(least, here))
-            least = jnp.minimum(least, here)
-        table[2 * o] = least
-        table[2 * o + 1] = second
-        return 0
-
-    lax.fori_loop(0, n_tile, fill, 0)
-
+    table_copy.wait()
     for copy in loads:
         copy.wait()
     pl.semaphore_wait(barrier, len(everyone))
@@ -120,14 +123,14 @@
             j = first + i // chunks
             row = low + (i % chunks) * CHUNK
             o = owner(j)
-            one_, two_ = table[2 * o], table[2 * o + 1]
+            one_, two_ = table[0, 0, o], table[1, 0, o]
             total = raw[pl.ds(one_ + row, CHUNK)].astype(f32) + raw[pl.ds(two_ + row, CHUNK)].astype(f32)
             store(j, pl.ds(row, CHUNK), total)
             return 0
 
         lax.fori_loop(0, count * chunks, one, 0)
 
-    x_copies, a1_copies, a2_copies, b2_copies, b_copies, d_copies = {}, {}, {}, {}, {}, {}
+    x_copies, a_copies, b2_copies, b_copies, d_copies = {}, {}, {}, {}, {}
 
     def rows_of(p):
         return pl.ds(BOUNDS[p], BOUNDS[p + 1] - BOUNDS[p])
@@ -136,51 +139,40 @@
         return lambda j: owner_of((a + step) % RING, (b + j) % RING, core)
 
     def to_partner(p):
-        for g, step in enumerate(GROUPS):
-
-            def keep(j, rows, total):
-                xs[g, j, rows] = total.astype(bf16)
-
-            spread(0, RING, p, lambda j: owner_of((b + step) % RING, (a + j) % RING, 1 - core), keep)
-            k = p * RING + g
-            x_copies[p, g] = send(
-                xs.at[g, :, rows_of(p)], xr.at[g, :, rows_of(p)], x_ss.at[k], x_rs.at[k], partner
+        for k, groups in enumerate(((0, 1, 2), (3,))):
+            for g in groups:
+
+                def keep(j, rows, total):
+                    xs[g, j, rows] = total.astype(bf16)
+
+                step = GROUPS[g]
+                spread(0, RING, p, lambda j: owner_of((b + step) % RING, (a + j) % RING, 1 - core), keep)
+            part, n = pl.ds(groups[0], len(groups)), p * 2 + k
+            x_copies[p, k] = send(
+                xs.at[part, :, rows_of(p)], xr.at[part, :, rows_of(p)], x_ss.at[n], x_rs.at[n], partner
             )
 
     def first_sends(p):
         x_copies[p, 0].wait_recv()
-
-        def keep(j, rows, total):
-            a1s[j, rows] = (total + xr[0, j, rows].astype(f32)).astype(bf16)
-
-        spread(0, RING, p, mine(2), keep)
         for way, device in enumerate((ahead, behind)):
+            for g, first in ((0, 2 * way), (1 + way, 2 - 2 * way)):
+
+                def keep(j, rows, total):
+                    as_[way, j, rows] = (total + xr[g, j, rows].astype(f32)).astype(bf16)
+
+                spread(first, 2, p, mine(GROUPS[g]), keep)
             k = p * 2 + way
-            part = pl.ds(2 * way, 2)
-            a1_copies[p, way] = send(
-                a1s.at[part, rows_of(p)], a1r.at[part, rows_of(p)], a1_ss.at[k], a1_rs.at[k], device
-            )
-        for way, device in enumerate((ahead, behind)):
-            g = 1 + way
-            x_copies[p, g].wait_recv()
-
-            def keep_far(j, rows, total):
-                a2s[j, rows] = (total + xr[g, j, rows].astype(f32)).astype(bf16)
-
-            spread(2 - 2 * way, 2, p, mine(GROUPS[g]), keep_far)
-            k = p * 2 + way
-            part = pl.ds(2 - 2 * way, 2)
-            a2_copies[p, way] = send(
-                a2s.at[part, rows_of(p)], a2r.at[part, rows_of(p)], a2_ss.at[k], a2_rs.at[k], device
+            a_copies[p, way] = send(
+                as_.at[way, :, rows_of(p)], ar.at[way, :, rows_of(p)], a_ss.at[k], a_rs.at[k], device
             )
 
     def second_sends(p):
         for way, device in enumerate((ahead, behind)):
             g = 1 + way
-            a1_copies[p, way].wait_recv()
+            a_copies[p, way].wait_recv()
 
             def keep(j, rows, total):
-                total = total + xr[g, j, rows].astype(f32) + a1r[j, rows].astype(f32)
+                total = total + xr[g, j, rows].astype(f32) + ar[way, j, rows].astype(f32)
                 b2s[j, rows] = total.astype(bf16)
 
             spread(2 * way, 2, p, mine(GROUPS[g]), keep)
@@ -191,14 +183,13 @@
             )
 
     def cross(p):
-        x_copies[p, 3].wait_recv()
+        x_copies[p, 1].wait_recv()
         for way in range(2):
-            a2_copies[p, way].wait_recv()
             b2_copies[p, way].wait_recv()
 
         def summed(j, rows, total):
             total = total + xr[3, j, rows].astype(f32)
-            return total + a2r[j, rows].astype(f32) + b2r[j, rows].astype(f32)
+            return total + ar[1 - j // 2, j, rows].astype(f32) + b2r[j, rows].astype(f32)
 
         def keep(j, rows, total):
             bs[j - 1, rows] = summed(j, rows, total).astype(bf16)
@@ -282,10 +273,9 @@
         lax.fori_loop(0, (high - low) // FILTER_CHUNK, one, 0)
 
     stages = (to_partner, first_sends, second_sends, cross, box, finish)
-    for t in range(pieces + len(stages) - 1):
-        for s, stage in enumerate(stages):
-            if 0 <= t - s < pieces:
-                stage(t - s)
+    steps = [(p + LAGS[s], (s if FIRST else -s), p, s) for p in range(pieces) for s in range(len(stages))]
+    for _, _, p, s in sorted(steps):
+        stages[s](p)
     for copy in sent:
         copy.wait_send()
 
@@ -308,17 +298,15 @@
     dma = pltpu.SemaphoreType.DMA
     scratch = [
         buffer(blocks * tile_rows + tile_rows),
-        pltpu.SMEM((2 * n_tile,), jnp.int32),
+        pltpu.VMEM((2, 8, 128), jnp.int32), pltpu.SMEM((2, 8, 128), jnp.int32),
         buffer(4, 4, tile_rows), buffer(4, 4, tile_rows),
-        buffer(4, tile_rows), buffer(4, tile_rows),
-        buffer(4, tile_rows), buffer(4, tile_rows),
+        buffer(2, 4, tile_rows), buffer(2, 4, tile_rows),
         buffer(4, tile_rows), buffer(4, tile_rows),
         buffer(3, tile_rows), buffer(3, tile_rows),
         buffer(tile_rows + 2 * HALF, dtype=f32),
         buffer(tile_rows, dtype=f32), buffer(tile_rows, dtype=f32),
         buffer(tile_rows), buffer(3, tile_rows),
-        dma((blocks,)), dma,
-        dma((pieces * 4,)), dma((pieces * 4,)),
+        dma((blocks,)), dma, dma,
         dma((pieces * 2,)), dma((pieces * 2,)),
         dma((pieces * 2,)), dma((pieces * 2,)),
         dma((pieces * 2,)), dma((pieces * 2,)),

time: 48.3 us -> 46.4 us (0.961)
  Pallas kernels: 46.3 us -> 44.4 us
    pallas_call x1, Pallas kernels: 46.3 us -> 44.4 us  [per_device(): pl.pallas_call(functools.partial(kernel, blocks, block_rows, tile_rows, n...]
where the time goes in v2:
time: 46.4 us; the launch traced here: 46.2 us
  Pallas kernels  44.4 us (96%)
  local copies, waits for them, and re-layouts  1.83 us (4%)
    pallas_call x1, Pallas kernels, per_device(): pl.pallas_call(functools.partial(kernel, blocks, block_rows, tile_rows, n...  44.4 us
    unnamed x1, local copies, waits for them, and re-layouts  1.83 us

profile of v2, /device:TPU:0, one launch (start us, length us, event | category | flops | bytes accessed | tf_op | source)
XLA Modules:
  0.0 46.2 jit_solution(13379013493152218930)
XLA Ops:
  0.0 44.4 %quegan.1 = bf16[128,8,128]{2,1,0:T(8,128)(2,1)} custom-call(bf16[1024,8,128]{2,1,0:T(8,128)(2,1)} %bitcast.16, s32[16]{0:T(128)} %bitcast.19, s32[16]{0:T(128)} %lead.1, f32[128,8,128]{2,1,0:T(8,128)} %bitcast.18), custom_call_target="tpu_custom_call" | custom-call | tf_op jit(solution)/shard_map/quegan/pallas_call | solution.py:316
  44.4 1.8 %copy.9 = bf16[1,128,2,512]{3,2,1,0:T(2,128)(2,1)} copy(bf16[1,128,2,512]{3,2,1,0:T(2,128)(2,1)} %bitcast.17) | data formatting | bytes 524288

commit v3 on v2

--- a/solution.py
+++ b/solution.py
@@ -9,14 +9,13 @@
 
 MESH = pl.DeviceIdType.MESH
 RING = 4
-BOUNDS = (0, 16, 32, 48, 64, 80, 96, 112, 128)
-LAGS = (0, 1, 4, 7, 9.5, 20)
-FIRST = True
-LAG = 4
+BOUNDS = (0, 8, 24, 40, 56, 72, 88, 104, 120, 128)
+LAGS = (0, 16, 64, 112, 152, 400)
+LAG = 8
 HALF = 3
 GROUPS = (2, 1, 3, 0)
 CHUNK = 16
-FILTER_CHUNK = 4
+FILTER_CHUNK = 8
 
 
 def owner_of(first, second, core):
@@ -117,15 +116,16 @@
 
     def spread(first, count, p, owner, store):
         low, high = BOUNDS[p], BOUNDS[p + 1]
-        chunks = (high - low) // CHUNK
+        chunk = min(CHUNK, high - low)
+        chunks = (high - low) // chunk
 
         def one(i, _):
             j = first + i // chunks
-            row = low + (i % chunks) * CHUNK
+            row = low + (i % chunks) * chunk
             o = owner(j)
             one_, two_ = table[0, 0, o], table[1, 0, o]
-            total = raw[pl.ds(one_ + row, CHUNK)].astype(f32) + raw[pl.ds(two_ + row, CHUNK)].astype(f32)
-            store(j, pl.ds(row, CHUNK), total)
+            total = raw[pl.ds(one_ + row, chunk)] + raw[pl.ds(two_ + row, chunk)]
+            store(j, pl.ds(row, chunk), total)
             return 0
 
         lax.fori_loop(0, count * chunks, one, 0)
@@ -143,7 +143,7 @@
             for g in groups:
 
                 def keep(j, rows, total):
-                    xs[g, j, rows] = total.astype(bf16)
+                    xs[g, j, rows] = total
 
                 step = GROUPS[g]
                 spread(0, RING, p, lambda j: owner_of((b + step) % RING, (a + j) % RING, 1 - core), keep)
@@ -158,7 +158,7 @@
             for g, first in ((0, 2 * way), (1 + way, 2 - 2 * way)):
 
                 def keep(j, rows, total):
-                    as_[way, j, rows] = (total + xr[g, j, rows].astype(f32)).astype(bf16)
+                    as_[way, j, rows] = total + xr[g, j, rows]
 
                 spread(first, 2, p, mine(GROUPS[g]), keep)
             k = p * 2 + way
@@ -172,8 +172,7 @@
             a_copies[p, way].wait_recv()
 
             def keep(j, rows, total):
-                total = total + xr[g, j, rows].astype(f32) + ar[way, j, rows].astype(f32)
-                b2s[j, rows] = total.astype(bf16)
+                b2s[j, rows] = (total + xr[g, j, rows]) + ar[way, j, rows]
 
             spread(2 * way, 2, p, mine(GROUPS[g]), keep)
             k = p * 2 + way
@@ -188,14 +187,14 @@
             b2_copies[p, way].wait_recv()
 
         def summed(j, rows, total):
-            total = total + xr[3, j, rows].astype(f32)
+            total = total.astype(f32) + xr[3, j, rows].astype(f32)
             return total + ar[1 - j // 2, j, rows].astype(f32) + b2r[j, rows].astype(f32)
 
         def keep(j, rows, total):
             bs[j - 1, rows] = summed(j, rows, total).astype(bf16)
 
         def keep_own(j, rows, total):
-            here = pl.ds(HALF + rows.start, CHUNK)
+            here = pl.ds(HALF + rows.start, rows.size)
             canvas[here] += summed(0, rows, total)
 
         spread(1, RING - 1, p, mine(0), keep)
@@ -219,14 +218,15 @@
         low, high = BOUNDS[p], BOUNDS[p + 1]
 
         def add(i, _):
-            row = low + i * CHUNK
-            rows = pl.ds(row, CHUNK)
-            canvas[pl.ds(HALF + row, CHUNK)] += (
+            row = low + i * step
+            rows = pl.ds(row, step)
+            canvas[pl.ds(HALF + row, step)] += (
                 br[0, rows].astype(f32) + br[1, rows].astype(f32) + br[2, rows].astype(f32)
             )
             return 0
 
-        lax.fori_loop(0, (high - low) // CHUNK, add, 0)
+        step = min(CHUNK, high - low)
+        lax.fori_loop(0, (high - low) // step, add, 0)
         low, high = filtered_rows(p)
         shape = (FILTER_CHUNK, 8, 128)
         column = (lax.broadcasted_iota(jnp.int32, shape, 1) // 2) * 128 + lax.broadcasted_iota(jnp.int32, shape, 2)
@@ -273,10 +273,14 @@
         lax.fori_loop(0, (high - low) // FILTER_CHUNK, one, 0)
 
     stages = (to_partner, first_sends, second_sends, cross, box, finish)
-    steps = [(p + LAGS[s], (s if FIRST else -s), p, s) for p in range(pieces) for s in range(len(stages))]
-    for _, _, p, s in sorted(steps):
+    steps = [(BOUNDS[p + 1] + LAGS[s], s, p) for p in range(pieces) for s in range(len(stages))]
+    steps.sort()
+    for _, s, p in steps[:-1]:
         stages[s](p)
-    for copy in sent:
+    for copy in sent[:-3]:
+        copy.wait_send()
+    finish(pieces - 1)
+    for copy in sent[-3:]:
         copy.wait_send()
 
 

time: 46.4 us -> 46.3 us (level)
  no operation moved by 1% of the time
where the time goes in v3:
time: 46.3 us; the launch traced here: 46.1 us
  Pallas kernels  44.2 us (95%)
  local copies, waits for them, and re-layouts  1.83 us (4%)
    pallas_call x1, Pallas kernels, per_device(): pl.pallas_call(functools.partial(kernel, blocks, block_rows, tile_rows, n...  44.2 us
    unnamed x1, local copies, waits for them, and re-layouts  1.83 us

profile of v3, /device:TPU:0, one launch (start us, length us, event | category | flops | bytes accessed | tf_op | source)
XLA Modules:
  0.0 46.1 jit_solution(924482785736080856)
XLA Ops:
  0.0 44.2 %quegan.1 = bf16[128,8,128]{2,1,0:T(8,128)(2,1)} custom-call(bf16[1024,8,128]{2,1,0:T(8,128)(2,1)} %bitcast.16, s32[16]{0:T(128)} %bitcast.19, s32[16]{0:T(128)} %lead.1, f32[128,8,128]{2,1,0:T(8,128)} %bitcast.18), custom_call_target="tpu_custom_call" | custom-call | tf_op jit(solution)/shard_map/quegan/pallas_call | solution.py:320
  44.3 1.8 %copy.9 = bf16[1,128,2,512]{3,2,1,0:T(2,128)(2,1)} copy(bf16[1,128,2,512]{3,2,1,0:T(2,128)(2,1)} %bitcast.17) | data formatting | bytes 524288

commit v4 on v3

--- a/solution.py
+++ b/solution.py
@@ -11,11 +11,11 @@
 RING = 4
 BOUNDS = (0, 8, 24, 40, 56, 72, 88, 104, 120, 128)
 LAGS = (0, 16, 64, 112, 152, 400)
-LAG = 8
+LAG = 4
 HALF = 3
 GROUPS = (2, 1, 3, 0)
 CHUNK = 16
-FILTER_CHUNK = 8
+FILTER_CHUNK = 4
 
 
 def owner_of(first, second, core):
@@ -102,7 +102,6 @@
     table_copy.wait()
     for copy in loads:
         copy.wait()
-    pl.semaphore_wait(barrier, len(everyone))
 
     sent = []
 
@@ -124,7 +123,7 @@
             row = low + (i % chunks) * chunk
             o = owner(j)
             one_, two_ = table[0, 0, o], table[1, 0, o]
-            total = raw[pl.ds(one_ + row, chunk)] + raw[pl.ds(two_ + row, chunk)]
+            total = raw[pl.ds(one_ + row, chunk)].astype(f32) + raw[pl.ds(two_ + row, chunk)].astype(f32)
             store(j, pl.ds(row, chunk), total)
             return 0
 
@@ -138,15 +137,19 @@
     def mine(step):
         return lambda j: owner_of((a + step) % RING, (b + j) % RING, core)
 
+    def build_for_partner(p, groups):
+        for g in groups:
+
+            def keep(j, rows, total):
+                xs[g, j, rows] = total.astype(bf16)
+
+            step = GROUPS[g]
+            spread(0, RING, p, lambda j: owner_of((b + step) % RING, (a + j) % RING, 1 - core), keep)
+
     def to_partner(p):
         for k, groups in enumerate(((0, 1, 2), (3,))):
-            for g in groups:
-
-                def keep(j, rows, total):
-                    xs[g, j, rows] = total
-
-                step = GROUPS[g]
-                spread(0, RING, p, lambda j: owner_of((b + step) % RING, (a + j) % RING, 1 - core), keep)
+            if p > 0:
+                build_for_partner(p, groups)
             part, n = pl.ds(groups[0], len(groups)), p * 2 + k
             x_copies[p, k] = send(
                 xs.at[part, :, rows_of(p)], xr.at[part, :, rows_of(p)], x_ss.at[n], x_rs.at[n], partner
@@ -158,7 +161,7 @@
             for g, first in ((0, 2 * way), (1 + way, 2 - 2 * way)):
 
                 def keep(j, rows, total):
-                    as_[way, j, rows] = total + xr[g, j, rows]
+                    as_[way, j, rows] = (total + xr[g, j, rows].astype(f32)).astype(bf16)
 
                 spread(first, 2, p, mine(GROUPS[g]), keep)
             k = p * 2 + way
@@ -172,7 +175,8 @@
             a_copies[p, way].wait_recv()
 
             def keep(j, rows, total):
-                b2s[j, rows] = (total + xr[g, j, rows]) + ar[way, j, rows]
+                total = total + xr[g, j, rows].astype(f32) + ar[way, j, rows].astype(f32)
+                b2s[j, rows] = total.astype(bf16)
 
             spread(2 * way, 2, p, mine(GROUPS[g]), keep)
             k = p * 2 + way
@@ -187,7 +191,7 @@
             b2_copies[p, way].wait_recv()
 
         def summed(j, rows, total):
-            total = total.astype(f32) + xr[3, j, rows].astype(f32)
+            total = total + xr[3, j, rows].astype(f32)
             return total + ar[1 - j // 2, j, rows].astype(f32) + b2r[j, rows].astype(f32)
 
         def keep(j, rows, total):
@@ -197,8 +201,8 @@
             here = pl.ds(HALF + rows.start, rows.size)
             canvas[here] += summed(0, rows, total)
 
-        spread(1, RING - 1, p, mine(0), keep)
         for j in (2, 1, 3):
+            spread(j, 1, p, mine(0), keep)
             k = p * 3 + j - 1
             b_copies[p, j] = send(
                 bs.at[j - 1, rows_of(p)], br.at[j - 1, rows_of(p)], b_ss.at[k], b_rs.at[k], across[j - 1]
@@ -272,6 +276,8 @@
 
         lax.fori_loop(0, (high - low) // FILTER_CHUNK, one, 0)
 
+    build_for_partner(0, range(RING))
+    pl.semaphore_wait(barrier, len(everyone))
     stages = (to_partner, first_sends, second_sends, cross, box, finish)
     steps = [(BOUNDS[p + 1] + LAGS[s], s, p) for p in range(pieces) for s in range(len(stages))]
     steps.sort()

time: 46.3 us -> 46.1 us (level)
  no operation moved by 1% of the time
where the time goes in v4:
time: 46.1 us; the launch traced here: 45.9 us
  Pallas kernels  44.1 us (96%)
  local copies, waits for them, and re-layouts  1.83 us (4%)
    pallas_call x1, Pallas kernels, per_device(): pl.pallas_call(functools.partial(kernel, blocks, block_rows, tile_rows, n...  44.1 us
    unnamed x1, local copies, waits for them, and re-layouts  1.83 us

profile of v4, /device:TPU:0, one launch (start us, length us, event | category | flops | bytes accessed | tf_op | source)
XLA Modules:
  0.0 45.9 jit_solution(12746849409885872750)
XLA Ops:
  0.0 44.1 %quegan.1 = bf16[128,8,128]{2,1,0:T(8,128)(2,1)} custom-call(bf16[1024,8,128]{2,1,0:T(8,128)(2,1)} %bitcast.16, s32[16]{0:T(128)} %bitcast.19, s32[16]{0:T(128)} %lead.1, f32[128,8,128]{2,1,0:T(8,128)} %bitcast.18), custom_call_target="tpu_custom_call" | custom-call | tf_op jit(solution)/shard_map/quegan/pallas_call | solution.py:326
  44.1 1.8 %copy.9 = bf16[1,128,2,512]{3,2,1,0:T(2,128)(2,1)} copy(bf16[1,128,2,512]{3,2,1,0:T(2,128)(2,1)} %bitcast.17) | data formatting | bytes 524288

commit v5 on v4

--- a/solution.py
+++ b/solution.py
@@ -147,7 +147,7 @@
             spread(0, RING, p, lambda j: owner_of((b + step) % RING, (a + j) % RING, 1 - core), keep)
 
     def to_partner(p):
-        for k, groups in enumerate(((0, 1, 2), (3,))):
+        for k, groups in enumerate(((0, 1), (2, 3))):
             if p > 0:
                 build_for_partner(p, groups)
             part, n = pl.ds(groups[0], len(groups)), p * 2 + k
@@ -156,8 +156,8 @@
             )
 
     def first_sends(p):
-        x_copies[p, 0].wait_recv()
         for way, device in enumerate((ahead, behind)):
+            x_copies[p, way].wait_recv()
             for g, first in ((0, 2 * way), (1 + way, 2 - 2 * way)):
 
                 def keep(j, rows, total):
@@ -186,7 +186,6 @@
             )
 
     def cross(p):
-        x_copies[p, 1].wait_recv()
         for way in range(2):
             b2_copies[p, way].wait_recv()
 

time: 46.1 us -> 45.7 us (level)
  no operation moved by 1% of the time
where the time goes in v5:
time: 45.7 us; the launch traced here: 45.6 us
  Pallas kernels  43.7 us (96%)
  local copies, waits for them, and re-layouts  1.83 us (4%)
    pallas_call x1, Pallas kernels, per_device(): pl.pallas_call(functools.partial(kernel, blocks, block_rows, tile_rows, n...  43.7 us
    unnamed x1, local copies, waits for them, and re-layouts  1.83 us

profile of v5, /device:TPU:0, one launch (start us, length us, event | category | flops | bytes accessed | tf_op | source)
XLA Modules:
  0.0 45.6 jit_solution(5391011898094923840)
XLA Ops:
  0.0 43.7 %quegan.1 = bf16[128,8,128]{2,1,0:T(8,128)(2,1)} custom-call(bf16[1024,8,128]{2,1,0:T(8,128)(2,1)} %bitcast.16, s32[16]{0:T(128)} %bitcast.19, s32[16]{0:T(128)} %lead.1, f32[128,8,128]{2,1,0:T(8,128)} %bitcast.18), custom_call_target="tpu_custom_call" | custom-call | tf_op jit(solution)/shard_map/quegan/pallas_call | solution.py:325
  43.7 1.8 %copy.9 = bf16[1,128,2,512]{3,2,1,0:T(2,128)(2,1)} copy(bf16[1,128,2,512]{3,2,1,0:T(2,128)(2,1)} %bitcast.17) | data formatting | bytes 524288
